TPU v7x, 32 devices: a whole 2x2x4 slice. The times are simulated.
32 devices in a mesh: group: 2 (over y), dp: 16 (over z, x, core).
Axes of the slice: x: 2, y: 2, z: 4, core: 2. Of those that a mesh axis runs over, the one named last changes fastest.
Arguments:
- queries: bfloat16 [8192, 4096], P(('group', 'dp')), parts along dimension 0, may hold values from -1024 to 1024
- keys: bfloat16 [8192, 512], P(('group', 'dp')), parts along dimension 0, may hold values from -8 to 8
- values: bfloat16 [8192, 512], P(('group', 'dp')), parts along dimension 0, may hold values from -6 to 6
- out_grad: bfloat16 [8192, 4096], P(('group', 'dp')), parts along dimension 0, may hold values from -6 to 6
- branch_ids: int32 [32, 256], P(('group', 'dp')), parts along dimension 0, may hold values from 0 to 3, never falling along the last dimension, each value on 1 to 128 neighbouring positions
- node_use: int32 [32, 4, 4], P(('group', 'dp')), parts along dimension 0, may hold values 0 or 1
Outputs:
- query_grad: bfloat16 [8192, 4096], P(('group', 'dp')), parts along dimension 0
- key_grad: bfloat16 [8192, 512], P(('group', 'dp')), parts along dimension 0
- value_grad: bfloat16 [8192, 512], P(('group', 'dp')), parts along dimension 0
There are 2 independent parts, one for each index of `group`. A program takes and returns all parts, laid end to end along the dimension named above; each array names one. Nothing has to cross between parts.
All inputs are finite; a program needn't handle non-finite values. No bound on the sum of `node_use` on one device may be relied on, other than what follows from the above.
Results may differ from a plain program's by a relative error of at most 0.015.
Values may be sent and summed in bfloat16 or wider, within the bound.
A program may use at most 192 MiB of HBM per device.

v0:
```python
import jax
import jax.numpy as jnp
from jax import lax
from jax.sharding import PartitionSpec as P

H = 32
KVH = 4
HD = 128
NODE_LEN = 128
REACH = 4
SEGS = 4


def from_behind(value, axis, steps):
    count = lax.axis_size(axis)
    pairs = [(source, (source + steps) % count) for source in range(count)]
    return lax.ppermute(value, axis, pairs)


def attention_backward(queries, key_all, value_all, out_grad, branch_row, use_table):
    tok_count = queries.shape[0]
    key_count = key_all.shape[0]
    groups = H // KVH
    scale = 1.0 / HD**0.5
    query_four = queries.reshape(tok_count, KVH, groups, HD)
    grad_four = out_grad.reshape(tok_count, KVH, groups, HD)
    key_three = key_all.reshape(key_count, KVH, HD)
    value_three = value_all.reshape(key_count, KVH, HD)
    position = jnp.arange(tok_count)
    local_mask = (branch_row[:, None] == branch_row[None, :]) & (
        position[None, :] <= position[:, None]
    )
    slot_onehot = (branch_row[:, None] == jnp.arange(SEGS)[None, :]).astype(jnp.float32)
    node_flags = (
        jnp.dot(slot_onehot, use_table.astype(jnp.float32), preferred_element_type=jnp.float32)
        > 0.5
    )
    node_mask = jnp.repeat(node_flags, NODE_LEN, axis=1)
    visible = jnp.concatenate([local_mask, node_mask], axis=1)
    scores = (
        jnp.einsum("tkgd,skd->kgts", query_four, key_three, preferred_element_type=jnp.float32)
        * scale
    )
    scores = jnp.where(visible[None, None], scores, -jnp.inf)
    norm_log = jax.nn.logsumexp(scores, axis=-1, keepdims=True)
    weights = jnp.exp(scores - norm_log)
    weight_low = weights.astype(jnp.bfloat16)
    value_terms = jnp.einsum(
        "kgts,tkgd->skd", weight_low, grad_four, preferred_element_type=jnp.float32
    )
    dprob = jnp.einsum("tkgd,skd->kgts", grad_four, value_three, preferred_element_type=jnp.float32)
    delta = jnp.sum(weights * dprob, axis=-1, keepdims=True)
    dscore = (weights * (dprob - delta)).astype(jnp.bfloat16)
    query_grad = (
        jnp.einsum("kgts,skd->tkgd", dscore, key_three, preferred_element_type=jnp.float32) * scale
    ).astype(jnp.bfloat16)
    key_terms = (
        jnp.einsum("kgts,tkgd->skd", dscore, query_four, preferred_element_type=jnp.float32) * scale
    )
    return (
        query_grad.reshape(tok_count, H * HD),
        key_terms.reshape(key_count, KVH * HD),
        value_terms.reshape(key_count, KVH * HD),
    )


def shards(queries, keys, values, out_grad, branch_ids, node_use):
    tok_count = queries.shape[0]
    width = keys.shape[1]
    node_pair = (keys[:NODE_LEN], values[:NODE_LEN])
    fetched_keys = []
    fetched_values = []
    for offset in range(REACH):
        arrived = from_behind((node_pair[0], node_pair[1]), "dp", offset + 1)
        fetched_keys.append(arrived[0])
        fetched_values.append(arrived[1])
    key_all = jnp.concatenate([keys] + fetched_keys, axis=0)
    value_all = jnp.concatenate([values] + fetched_values, axis=0)
    query_grad, key_terms, value_terms = attention_backward(
        queries, key_all, value_all, out_grad, branch_ids[0], node_use[0]
    )
    node_keys = key_terms[tok_count:].reshape(REACH, NODE_LEN, width)
    node_values = value_terms[tok_count:].reshape(REACH, NODE_LEN, width)
    carry_key = jnp.zeros((NODE_LEN, width), jnp.float32)
    carry_value = jnp.zeros((NODE_LEN, width), jnp.float32)
    for offset in range(REACH):
        moved = (
            from_behind(node_keys[offset].astype(jnp.bfloat16), "dp", -(offset + 1)).astype(
                jnp.float32
            ),
            from_behind(node_values[offset].astype(jnp.bfloat16), "dp", -(offset + 1)).astype(
                jnp.float32
            ),
        )
        carry_key = carry_key + moved[0]
        carry_value = carry_value + moved[1]
    key_grad = key_terms[:tok_count].at[:NODE_LEN].add(carry_key).astype(jnp.bfloat16)
    value_grad = value_terms[:tok_count].at[:NODE_LEN].add(carry_value).astype(jnp.bfloat16)
    return (query_grad, key_grad, value_grad)


def solution(mesh):
    placed = (
        P(("group", "dp"), None),
        P(("group", "dp"), None),
        P(("group", "dp"), None),
        P(("group", "dp"), None),
        P(("group", "dp"), None),
        P(("group", "dp"), None, None),
    )
    return jax.shard_map(
        shards,
        mesh=mesh,
        in_specs=placed,
        out_specs=(P(("group", "dp"), None), P(("group", "dp"), None), P(("group", "dp"), None)),
        check_vma=False,
    )
```

profile of v0, /device:TPU:0, one launch (start us, length us, event | category | flops | bytes accessed | tf_op | source)
XLA Modules:
  0.0 150.2 jit_solution(14354648675188799985)
XLA Ops:
  0.6 1.1 copy.31
  1.7 3.1 %collective-permute-start.3 = (bf16[128,512]{0,1:T(8,128)(2,1)S(1)}, bf16[128,512]{0,1:T(8,128)(2,1)S(1)}, u32[]{:S(2)}, u32[]{:S(2)}) collective-permute-start(bf16[128,512]{0,1:T(8,128)(2,1)S(1)} %slice.128), channel_id=1, source_target_pairs={{0,4},{1,5},{2,6},{3,7},{4,8},{5,9},{6,10},{7,11},{8,12},{9,13},{1... | collective-permute-start | bytes 393224 | tf_op jit(solution)/shard_map/ppermute | solution.py:17
  5.5 1.5 %collective-permute-start.1 = (bf16[128,512]{0,1:T(8,128)(2,1)S(1)}, bf16[128,512]{0,1:T(8,128)(2,1)}, u32[]{:S(2)}, u32[]{:S(2)}) collective-permute-start(bf16[128,512]{0,1:T(8,128)(2,1)S(1)} %slice.128), channel_id=1, source_target_pairs={{0,2},{1,3},{2,4},{3,5},{4,6},{5,7},{6,8},{7,9},{8,10},{9,11},{10,... | collective-permute-start | bytes 393224 | tf_op jit(solution)/shard_map/ppermute | solution.py:17
  7.7 1.1 copy.35
  9.5 1.6 %collective-permute-start.7 = (bf16[128,512]{0,1:T(8,128)(2,1)}, bf16[128,512]{0,1:T(8,128)(2,1)S(1)}, u32[]{:S(2)}, u32[]{:S(2)}) collective-permute-start(bf16[128,512]{0,1:T(8,128)(2,1)} %slice.129), channel_id=1, source_target_pairs={{0,4},{1,5},{2,6},{3,7},{4,8},{5,9},{6,10},{7,11},{8,12},{9,13},{1... | collective-permute-start | bytes 393224 | tf_op jit(solution)/shard_map/ppermute | solution.py:17
  13.7 3.3 %copy.68 = bf16[256,4096]{0,1:T(8,128)(2,1)S(1)} copy(bf16[256,4096]{1,0:T(8,128)(2,1)} %param.10) | data formatting | bytes 4194304 | tf_op jit(solution)/shard_map/reshape | solution.py:25
  17.0 4.1 %copy.69 = bf16[256,4096]{0,1:T(8,128)(2,1)} copy(bf16[256,4096]{1,0:T(8,128)(2,1)} %param.13) | data formatting | bytes 4194304 | tf_op jit(solution)/shard_map/reshape | solution.py:26
  21.0 1.1 collective-permute-start.6
  22.1 0.9 constant_dynamic-update-slice_fusion.3
  23.1 1.0 collective-permute-start.5
  24.1 0.9 constant_dynamic-update-slice_fusion.2
  25.1 0.9 constant_dynamic-update-slice_fusion.1
  26.1 10.3 %fusion.4 = (f32[4,8,256]{2,1,0:T(8,128)S(1)}, f32[4,768,256,8]{2,1,3,0:T(8,128)}) fusion(pred[256,768]{0,1:T(8,128)(4,1)S(1)} %pad_add_fusion, bf16[768,4,128,1]{0,2,3,1:T(8,128)(2,1)S(1)} %bitcast.87, bf16[256,4,8,128]{0,3,2,1:T(8,128)(2,1)S(1)} %bitcast.82), kind=kOutput, calls=%fused_computation.9 | convolution fusion | flops 1629478912 | bytes 28278784 | tf_op jit(solution)/shard_map/tkgd,skd->kgts/dot_general | solution.py:41
  36.4 11.1 %exponential_reduce_fusion = f32[4,8,256]{2,1,0:T(8,128)S(1)} fusion(f32[4,768,256,8]{2,1,3,0:T(8,128)} %get-tuple-element.42, f32[4,8,256]{2,1,0:T(8,128)S(1)} %is-finite_select_fusion, pred[256,768]{0,1:T(8,128)(4,1)S(1)} %pad_add_fusion), kind=kLoop, calls=%fused_computation.7 | loop fusion | flops 25157632 | bytes 25427968 | tf_op jit(solution)/shard_map/reduce_sum | solution.py:45
  47.5 12.2 %fusion.21 = (bf16[768,4,128]{0,2,1:T(8,128)(2,1)}, f32[768,4,128]{0,2,1:T(8,128)S(1)}) fusion(bf16[256,4,8,128]{0,3,2,1:T(8,128)(2,1)S(1)} %bitcast.85, f32[4,768,256,8]{2,1,3,0:T(8,128)} %get-tuple-element.42, f32[4,8,256]{2,1,0:T(8,128)S(1)} %log_add_fusion, pred[256,768]{0,1:T(8,128)(4,1)S(1)} %pad_add_fusion), kind=kOutput, calls=%fused_computation.43 | convolution fusion | flops 1636171776 | bytes 29851648 | tf_op jit(solution)/shard_map/kgts,tkgd->skd/dot_general | solution.py:48
  63.3 17.2 %fusion = (f32[4,8,256]{2,1,0:T(8,128)S(1)}, f32[4,768,256,8]{2,1,3,0:T(8,128)}) fusion(f32[4,768,256,8]{2,1,3,0:T(8,128)} %get-tuple-element.42, f32[4,8,256]{2,1,0:T(8,128)S(1)} %log_add_fusion, pred[256,768]{0,1:T(8,128)(4,1)S(1)} %pad_add_fusion, bf16[768,4,128,1]{0,2,3,1:T(8,128)(2,1)} %bitcast.36, bf16[256,4,8,128]{0,3,2,1:T(8,128)(2,1)} %bitcast.84), kind=kOutput, calls=%fused_computation.2 | convolution fusion | flops 1642061824 | bytes 53477376 | tf_op jit(solution)/shard_map/tkgd,skd->kgts/dot_general | solution.py:51
  80.5 21.7 %fusion.2 = bf16[4,8,256,768]{2,3,1,0:T(8,128)(2,1)} fusion(f32[4,768,256,8]{2,1,3,0:T(8,128)} %get-tuple-element.44, f32[4,768,256,8]{2,1,3,0:T(8,128)} %get-tuple-element.42, f32[4,8,256]{2,1,0:T(8,128)S(1)} %get-tuple-element.43, f32[4,8,256]{2,1,0:T(8,128)S(1)} %log_add_fusion, pred[256,768]{0,1:T(8,128)(4,1)S(1)} %pad_add_fusion), kind=kLoop, calls=%fused_computation.4 | loop fusion | flops 37748736 | bytes 63176704 | tf_op jit(solution)/shard_map/convert_element_type | solution.py:53
  102.2 10.1 %fusion.20 = (bf16[768,4,128]{0,2,1:T(8,128)(2,1)}, f32[768,4,128]{0,2,1:T(8,128)}) fusion(bf16[4,8,256,768]{2,3,1,0:T(8,128)(2,1)} %fusion.2, bf16[256,4,8,128]{0,3,2,1:T(8,128)(2,1)S(1)} %bitcast.83), kind=kOutput, calls=%fused_computation.42 | convolution fusion | flops 1611399168 | bytes 17039360 | tf_op jit(solution)/shard_map/kgts,tkgd->skd/dot_general | solution.py:58
  112.4 6.4 %multiply_convert_fusion = bf16[4,128,8,256]{3,1,2,0:T(8,128)(2,1)S(1)} fusion(bf16[768,4,128,1]{0,2,3,1:T(8,128)(2,1)S(1)} %bitcast.88, bf16[4,8,256,768]{2,3,1,0:T(8,128)(2,1)} %fusion.2), kind=kOutput, calls=%fused_computation.12 | convolution fusion | flops 1612709888 | bytes 15466496 | tf_op jit(solution)/shard_map/kgts,skd->tkgd/dot_general | solution.py:55
  118.8 1.0 slice.131
  119.7 1.1 slice.130
  120.8 1.1 fusion.18
  124.4 3.8 %collective-permute-start.13 = (bf16[128,512]{1,0:T(8,128)(2,1)}, bf16[128,512]{1,0:T(8,128)(2,1)}, u32[]{:S(2)}, u32[]{:S(2)}) collective-permute-start(bf16[128,512]{1,0:T(8,128)(2,1)} %copy.50), channel_id=1, source_target_pairs={{0,14},{1,15},{2,0},{3,1},{4,2},{5,3},{6,4},{7,5},{8,6},{9,7},{10,... | collective-permute-start | bytes 393224 | tf_op jit(solution)/shard_map/ppermute | solution.py:17
  128.1 2.1 %collective-permute-start.14 = (bf16[128,512]{1,0:T(8,128)(2,1)}, bf16[128,512]{1,0:T(8,128)(2,1)}, u32[]{:S(2)}, u32[]{:S(2)}) collective-permute-start(bf16[128,512]{1,0:T(8,128)(2,1)} %copy.51), channel_id=1, source_target_pairs={{0,13},{1,14},{2,15},{3,0},{4,1},{5,2},{6,3},{7,4},{8,5},{9,6},{10... | collective-permute-start | bytes 393224 | tf_op jit(solution)/shard_map/ppermute | solution.py:17
  130.6 1.8 %copy.54 = bf16[256,512]{1,0:T(8,128)(2,1)} copy(bf16[256,512]{0,1:T(8,128)(2,1)} %bitcast.90) | data formatting | bytes 524288 | tf_op jit(solution)/shard_map/slice | solution.py:98
  132.6 1.1 fusion.19
  134.6 2.9 %copy.55 = bf16[256,4096]{1,0:T(8,128)(2,1)} copy(bf16[256,4096]{0,1:T(8,128)(2,1)S(1)} %bitcast.86) | data formatting | bytes 4194304
  137.7 1.3 collective-permute-start.9
  139.4 2.5 %collective-permute-start.11 = (bf16[128,512]{1,0:T(8,128)(2,1)S(1)}, bf16[128,512]{1,0:T(8,128)(2,1)S(1)}, u32[]{:S(2)}, u32[]{:S(2)}) collective-permute-start(bf16[128,512]{1,0:T(8,128)(2,1)S(1)} %copy.44), channel_id=1, source_target_pairs={{0,12},{1,13},{2,14},{3,15},{4,0},{5,1},{6,2},{7,3},{8,4},{9,5},{1... | collective-permute-start | bytes 393224 | tf_op jit(solution)/shard_map/ppermute | solution.py:17
  141.8 1.7 %collective-permute-start.8 = (bf16[128,512]{1,0:T(8,128)(2,1)}, bf16[128,512]{1,0:T(8,128)(2,1)S(1)}, u32[]{:S(2)}, u32[]{:S(2)}) collective-permute-start(bf16[128,512]{1,0:T(8,128)(2,1)} %copy.41), channel_id=1, source_target_pairs={{0,15},{1,0},{2,1},{3,2},{4,3},{5,4},{6,5},{7,6},{8,7},{9,8},{10,9... | collective-permute-start | bytes 393224 | tf_op jit(solution)/shard_map/ppermute | solution.py:17
  143.5 1.8 %add_dynamic-update-slice_fusion = bf16[256,512]{1,0:T(8,128)(2,1)} fusion(bf16[256,512]{1,0:T(8,128)(2,1)} %copy.54, f32[128,512]{1,0:T(8,128)S(1)} %copy.53, bf16[128,512]{1,0:T(8,128)(2,1)} %collective-permute-done.15, bf16[128,512]{1,0:T(8,128)(2,1)} %collective-permute-done.14, bf16[128,512]{1,0:T(8,128)(2,1)} %collective-permute-done.13, ...), kind=kLoop, calls=%fused_computation.18 | loop fusion | flops 524288 | bytes 1048576 | tf_op jit(solution)/shard_map/scatter-add | solution.py:98
  145.7 3.7 %collective-permute-done.11 = bf16[128,512]{1,0:T(8,128)(2,1)S(1)} collective-permute-done((bf16[128,512]{1,0:T(8,128)(2,1)S(1)}, bf16[128,512]{1,0:T(8,128)(2,1)S(1)}, u32[]{:S(2)}, u32[]{:S(2)}) %collective-permute-start.11) | collective-permute-done | bytes 131104 | tf_op jit(solution)/shard_map/ppermute | solution.py:17
  (54 shorter events, 13.8 us)
Async XLA Ops:
  1.7 24.3 %collective-permute-start.3 = (bf16[128,512]{0,1:T(8,128)(2,1)S(1)}, bf16[128,512]{0,1:T(8,128)(2,1)S(1)}, u32[]{:S(2)}, u32[]{:S(2)}) collective-permute-start(bf16[128,512]{0,1:T(8,128)(2,1)S(1)} %slice.128), channel_id=1, source_target_pairs={{0,4},{1,5},{2,6},{3,7},{4,8},{5,9},{6,10},{7,11},{8,12},{9,13},{1... | collective-permute-start | bytes 393224 | tf_op jit(solution)/shard_map/ppermute | solution.py:17
  4.8 20.2 %collective-permute-start.2 = (bf16[128,512]{0,1:T(8,128)(2,1)S(1)}, bf16[128,512]{0,1:T(8,128)(2,1)}, u32[]{:S(2)}, u32[]{:S(2)}) collective-permute-start(bf16[128,512]{0,1:T(8,128)(2,1)S(1)} %slice.128), channel_id=1, source_target_pairs={{0,3},{1,4},{2,5},{3,6},{4,7},{5,8},{6,9},{7,10},{8,11},{9,12},{10... | collective-permute-start | bytes 393224 | tf_op jit(solution)/shard_map/ppermute | solution.py:17
  5.5 17.6 %collective-permute-start.1 = (bf16[128,512]{0,1:T(8,128)(2,1)S(1)}, bf16[128,512]{0,1:T(8,128)(2,1)}, u32[]{:S(2)}, u32[]{:S(2)}) collective-permute-start(bf16[128,512]{0,1:T(8,128)(2,1)S(1)} %slice.128), channel_id=1, source_target_pairs={{0,2},{1,3},{2,4},{3,5},{4,6},{5,7},{6,8},{7,9},{8,10},{9,11},{10,... | collective-permute-start | bytes 393224 | tf_op jit(solution)/shard_map/ppermute | solution.py:17
  7.0 14.0 %collective-permute-start = (bf16[128,512]{0,1:T(8,128)(2,1)S(1)}, bf16[128,512]{0,1:T(8,128)(2,1)}, u32[]{:S(2)}, u32[]{:S(2)}) collective-permute-start(bf16[128,512]{0,1:T(8,128)(2,1)S(1)} %slice.128), channel_id=1, source_target_pairs={{0,1},{1,2},{2,3},{3,4},{4,5},{5,6},{6,7},{7,8},{8,9},{9,10},{10,1... | collective-permute-start | bytes 393224 | tf_op jit(solution)/shard_map/ppermute | solution.py:17
  9.5 53.1 %collective-permute-start.7 = (bf16[128,512]{0,1:T(8,128)(2,1)}, bf16[128,512]{0,1:T(8,128)(2,1)S(1)}, u32[]{:S(2)}, u32[]{:S(2)}) collective-permute-start(bf16[128,512]{0,1:T(8,128)(2,1)} %slice.129), channel_id=1, source_target_pairs={{0,4},{1,5},{2,6},{3,7},{4,8},{5,9},{6,10},{7,11},{8,12},{9,13},{1... | collective-permute-start | bytes 393224 | tf_op jit(solution)/shard_map/ppermute | solution.py:17
  21.0 40.9 %collective-permute-start.6 = (bf16[128,512]{0,1:T(8,128)(2,1)}, bf16[128,512]{0,1:T(8,128)(2,1)S(1)}, u32[]{:S(2)}, u32[]{:S(2)}) collective-permute-start(bf16[128,512]{0,1:T(8,128)(2,1)} %slice.129), channel_id=1, source_target_pairs={{0,3},{1,4},{2,5},{3,6},{4,7},{5,8},{6,9},{7,10},{8,11},{9,12},{10... | collective-permute-start | bytes 393224 | tf_op jit(solution)/shard_map/ppermute | solution.py:17
  23.1 37.4 %collective-permute-start.5 = (bf16[128,512]{0,1:T(8,128)(2,1)}, bf16[128,512]{0,1:T(8,128)(2,1)S(1)}, u32[]{:S(2)}, u32[]{:S(2)}) collective-permute-start(bf16[128,512]{0,1:T(8,128)(2,1)} %slice.129), channel_id=1, source_target_pairs={{0,2},{1,3},{2,4},{3,5},{4,6},{5,7},{6,8},{7,9},{8,10},{9,11},{10,... | collective-permute-start | bytes 393224 | tf_op jit(solution)/shard_map/ppermute | solution.py:17
  25.0 34.8 %collective-permute-start.4 = (bf16[128,512]{0,1:T(8,128)(2,1)}, bf16[128,512]{0,1:T(8,128)(2,1)S(1)}, u32[]{:S(2)}, u32[]{:S(2)}) collective-permute-start(bf16[128,512]{0,1:T(8,128)(2,1)} %slice.129), channel_id=1, source_target_pairs={{0,1},{1,2},{2,3},{3,4},{4,5},{5,6},{6,7},{7,8},{8,9},{9,10},{10,1... | collective-permute-start | bytes 393224 | tf_op jit(solution)/shard_map/ppermute | solution.py:17
  26.1 21.5 %copy-start = (bf16[256,4096]{0,1:T(8,128)(2,1)S(1)}, bf16[256,4096]{0,1:T(8,128)(2,1)}, u32[]{:S(2)}) copy-start(bf16[256,4096]{0,1:T(8,128)(2,1)} %copy.69) | copy-start | bytes 6291460
  124.4 14.9 %collective-permute-start.13 = (bf16[128,512]{1,0:T(8,128)(2,1)}, bf16[128,512]{1,0:T(8,128)(2,1)}, u32[]{:S(2)}, u32[]{:S(2)}) collective-permute-start(bf16[128,512]{1,0:T(8,128)(2,1)} %copy.50), channel_id=1, source_target_pairs={{0,14},{1,15},{2,0},{3,1},{4,2},{5,3},{6,4},{7,5},{8,6},{9,7},{10,... | collective-permute-start | bytes 393224 | tf_op jit(solution)/shard_map/ppermute | solution.py:17
  128.1 11.2 %collective-permute-start.14 = (bf16[128,512]{1,0:T(8,128)(2,1)}, bf16[128,512]{1,0:T(8,128)(2,1)}, u32[]{:S(2)}, u32[]{:S(2)}) collective-permute-start(bf16[128,512]{1,0:T(8,128)(2,1)} %copy.51), channel_id=1, source_target_pairs={{0,13},{1,14},{2,15},{3,0},{4,1},{5,2},{6,3},{7,4},{8,5},{9,6},{10... | collective-permute-start | bytes 393224 | tf_op jit(solution)/shard_map/ppermute | solution.py:17
  130.2 11.6 %collective-permute-start.15 = (bf16[128,512]{1,0:T(8,128)(2,1)S(1)}, bf16[128,512]{1,0:T(8,128)(2,1)}, u32[]{:S(2)}, u32[]{:S(2)}) collective-permute-start(bf16[128,512]{1,0:T(8,128)(2,1)S(1)} %copy.52), channel_id=1, source_target_pairs={{0,12},{1,13},{2,14},{3,15},{4,0},{5,1},{6,2},{7,3},{8,4},{9,5},{1... | collective-permute-start | bytes 393224 | tf_op jit(solution)/shard_map/ppermute | solution.py:17
  130.6 12.9 %collective-permute-start.12 = (bf16[128,512]{1,0:T(8,128)(2,1)}, bf16[128,512]{1,0:T(8,128)(2,1)}, u32[]{:S(2)}, u32[]{:S(2)}) collective-permute-start(bf16[128,512]{1,0:T(8,128)(2,1)} %copy.49), channel_id=1, source_target_pairs={{0,15},{1,0},{2,1},{3,2},{4,3},{5,4},{6,5},{7,6},{8,7},{9,8},{10,9... | collective-permute-start | bytes 393224 | tf_op jit(solution)/shard_map/ppermute | solution.py:17
  137.7 7.7 %collective-permute-start.9 = (bf16[128,512]{1,0:T(8,128)(2,1)S(1)}, bf16[128,512]{1,0:T(8,128)(2,1)S(1)}, u32[]{:S(2)}, u32[]{:S(2)}) collective-permute-start(bf16[128,512]{1,0:T(8,128)(2,1)S(1)} %copy.42), channel_id=1, source_target_pairs={{0,14},{1,15},{2,0},{3,1},{4,2},{5,3},{6,4},{7,5},{8,6},{9,7},{10,... | collective-permute-start | bytes 393224 | tf_op jit(solution)/shard_map/ppermute | solution.py:17
  139.3 6.4 %collective-permute-start.10 = (bf16[128,512]{1,0:T(8,128)(2,1)S(1)}, bf16[128,512]{1,0:T(8,128)(2,1)S(1)}, u32[]{:S(2)}, u32[]{:S(2)}) collective-permute-start(bf16[128,512]{1,0:T(8,128)(2,1)S(1)} %copy.43), channel_id=1, source_target_pairs={{0,13},{1,14},{2,15},{3,0},{4,1},{5,2},{6,3},{7,4},{8,5},{9,6},{10... | collective-permute-start | bytes 393224 | tf_op jit(solution)/shard_map/ppermute | solution.py:17
  139.4 10.0 %collective-permute-start.11 = (bf16[128,512]{1,0:T(8,128)(2,1)S(1)}, bf16[128,512]{1,0:T(8,128)(2,1)S(1)}, u32[]{:S(2)}, u32[]{:S(2)}) collective-permute-start(bf16[128,512]{1,0:T(8,128)(2,1)S(1)} %copy.44), channel_id=1, source_target_pairs={{0,12},{1,13},{2,14},{3,15},{4,0},{5,1},{6,2},{7,3},{8,4},{9,5},{1... | collective-permute-start | bytes 393224 | tf_op jit(solution)/shard_map/ppermute | solution.py:17
  141.8 7.5 %collective-permute-start.8 = (bf16[128,512]{1,0:T(8,128)(2,1)}, bf16[128,512]{1,0:T(8,128)(2,1)S(1)}, u32[]{:S(2)}, u32[]{:S(2)}) collective-permute-start(bf16[128,512]{1,0:T(8,128)(2,1)} %copy.41), channel_id=1, source_target_pairs={{0,15},{1,0},{2,1},{3,2},{4,3},{5,4},{6,5},{7,6},{8,7},{9,8},{10,9... | collective-permute-start | bytes 393224 | tf_op jit(solution)/shard_map/ppermute | solution.py:17
  149.5 0.7 copy-start.1
where the time goes:
time: 151 us; the launch traced here: 150 us
  matrix products  57.2 us (38%)
  other arithmetic  35.6 us (24%)
  local copies, waits for them, and re-layouts  30.9 us (20%)
  starting transfers between devices  21.5 us (14%)
  waiting for transfers between devices  4.04 us (3%)
    convert_element_type x1, other arithmetic, attention_backward(): dscore = (weights * (dprob - delta)).astype(jnp.bfloat16)  21.7 us
    ppermute x16, starting transfers between devices, from_behind(): return lax.ppermute(value, axis, pairs)  21.5 us
    dot_general x1, matrix products, attention_backward(): jnp.einsum('tkgd,skd->kgts', grad_four, value_three, preferred_element_ty...  17.2 us
    dot_general x1, matrix products, attention_backward(): jnp.einsum('kgts,tkgd->skd', weight_low, grad_four, preferred_element_typ...  12.2 us
    unnamed x15, local copies, waits for them, and re-layouts  11.4 us
    reduce_sum x1, other arithmetic, attention_backward(): norm_log = jax.nn.logsumexp(scores, axis=-1, keepdims=True)  11.1 us
    dot_general x1, matrix products, attention_backward(): jnp.einsum('tkgd,skd->kgts', query_four, key_three, preferred_element_typ...  10.3 us
    dot_general x1, matrix products, attention_backward(): jnp.einsum('kgts,tkgd->skd', dscore, query_four, preferred_element_type=j...  10.1 us
  transfers between devices with their start and end apart: 16, of which 2 were waited for; matrix products, arithmetic and copies ran while one was open for 40% of the time, Pallas kernels for 0%

commit v1 on v0

v1 whole, which is shorter than its diff:
```python
import math

import jax
import jax.numpy as jnp
from jax import lax
from jax.experimental import pallas as pl
from jax.experimental.pallas import tpu as pltpu
from jax.sharding import PartitionSpec as P

H = 32
KVH = 4
HD = 128
NODE_LEN = 128
REACH = 4
SEGS = 4
GROUPS = H // KVH
UNROLL = 2
HIDDEN = -1e30
MESH = pl.DeviceIdType.MESH


def fill_bias(branch_ref, use_ref, bias):
    tok = branch_ref.shape[1]
    row = branch_ref[...]
    key_branch = jnp.broadcast_to(row.astype(jnp.float32), (tok, tok)).T
    query_branch = jnp.broadcast_to(row.astype(jnp.float32), (tok, tok))
    key_at = lax.broadcasted_iota(jnp.int32, (tok, tok), 0)
    query_at = lax.broadcasted_iota(jnp.int32, (tok, tok), 1)
    local = (key_branch == query_branch) & (key_at <= query_at)
    bias[0:tok, :] = jnp.where(local, 0.0, HIDDEN)
    for r in range(REACH):
        flag = jnp.zeros((1, tok), jnp.int32)
        for slot in range(SEGS):
            flag = jnp.where(row == slot, use_ref[0, slot, r], flag)
        line = jnp.where(flag > 0, 0.0, HIDDEN).astype(jnp.float32)
        bias[tok + r * NODE_LEN : tok + (r + 1) * NODE_LEN, :] = jnp.broadcast_to(
            line, (NODE_LEN, tok)
        )


def kernel(
    q_hbm, k_hbm, v_hbm, g_hbm, branch_ref, use_ref,
    dq_hbm, dk_hbm, dv_hbm,
    q_s, g_s, dq_s, k_s, v_s, dk_s, dv_s, bias, back_out, back_in, dk_o, dv_o,
    in_sem, out_sem, k_send, k_recv, v_send, v_recv, back_send, back_recv,
):
    count = lax.axis_size("dp")
    me = lax.axis_index("dp")
    group = lax.axis_index("group")
    tok = q_hbm.shape[0]
    wide = GROUPS * HD
    scale = 1.0 / HD**0.5
    scale2 = scale * math.log2(math.e)

    def ahead(steps):
        return (group, lax.rem(me + steps + count, count))

    def cols(a, width):
        return pl.ds(pl.multiple_of(a * width, width), width)

    def load(a, which):
        if which < 2:
            source, target = ((q_hbm, q_s), (g_hbm, g_s))[which]
            return pltpu.make_async_copy(
                source.at[:, cols(a, wide)], target.at[:, cols(a, wide)], in_sem.at[which, a]
            )
        source, target = ((k_hbm, k_s), (v_hbm, v_s))[which - 2]
        return pltpu.make_async_copy(
            source.at[:, cols(a, HD)], target.at[a, pl.ds(0, tok)], in_sem.at[which, a]
        )

    def forward(a, r, which):
        source, target, send, recv = (
            (k_hbm, k_s, k_send, k_recv),
            (v_hbm, v_s, v_send, v_recv),
        )[which]
        return pltpu.make_async_remote_copy(
            src_ref=source.at[pl.ds(0, NODE_LEN), cols(a, HD)],
            dst_ref=target.at[a, pl.ds(tok + r * NODE_LEN, NODE_LEN)],
            send_sem=send.at[a, r],
            recv_sem=recv.at[a, r],
            device_id=ahead(r + 1),
            device_id_type=MESH,
        )

    def back(a, r):
        return pltpu.make_async_remote_copy(
            src_ref=back_out.at[a, r],
            dst_ref=back_in.at[a, r],
            send_sem=back_send.at[a, r],
            recv_sem=back_recv.at[a, r],
            device_id=ahead(-(r + 1)),
            device_id_type=MESH,
        )

    def store_query(a):
        return pltpu.make_async_copy(
            dq_s.at[:, cols(a, wide)], dq_hbm.at[:, cols(a, wide)], out_sem.at[a]
        )

    @pl.loop(0, KVH)
    def _(a):
        for which in range(4):
            load(a, which).start()

    barrier = pltpu.get_barrier_semaphore()
    for r in range(REACH):
        for side in (r + 1, -(r + 1)):
            pl.semaphore_signal(barrier, inc=1, device_id=ahead(side), device_id_type=MESH)
    pl.semaphore_wait(barrier, 2 * REACH)

    @pl.loop(0, KVH)
    def _(a):
        for r in range(REACH):
            for which in range(2):
                forward(a, r, which).start()

    fill_bias(branch_ref, use_ref, bias)

    @pl.loop(0, KVH)
    def _(a):
        for which in range(4):
            load(a, which).wait()
        for r in range(REACH):
            for which in range(2):
                forward(a, r, which).wait()
        dk_s[a] = jnp.zeros(dk_s.shape[1:], jnp.float32)
        dv_s[a] = jnp.zeros(dv_s.shape[1:], jnp.float32)
        key = k_s[a]
        value = v_s[a]
        key_turned = key.T

        def one_head(b):
            at = cols(a * GROUPS + b, HD)
            query = q_s[:, at]
            grad = g_s[:, at]
            scores = lax.dot_general(
                key, query, (((1,), (1,)), ((), ())), preferred_element_type=jnp.float32
            )
            scores = scores * scale2 + bias[...]
            dprob = lax.dot_general(
                value, grad, (((1,), (1,)), ((), ())), preferred_element_type=jnp.float32
            )
            top = jnp.max(scores, axis=0, keepdims=True)
            power = jnp.exp2(scores - top)
            total = jnp.sum(power, axis=0, keepdims=True)
            share = 1.0 / total
            delta = jnp.sum(power * dprob, axis=0, keepdims=True) * share
            weights = power * share
            dscore = (weights * (dprob - delta)).astype(jnp.bfloat16)
            dv = jnp.dot(weights.astype(jnp.bfloat16), grad, preferred_element_type=jnp.float32)
            dk = jnp.dot(dscore, query, preferred_element_type=jnp.float32)
            dq = jnp.dot(key_turned, dscore, preferred_element_type=jnp.float32)
            dq_s[:, at] = (dq * scale).T.astype(jnp.bfloat16)
            return dk, dv

        @pl.loop(0, GROUPS // UNROLL)
        def _(pair):
            parts = [one_head(pair * UNROLL + i) for i in range(UNROLL)]
            dk, dv = parts[0]
            for more in parts[1:]:
                dk = dk + more[0]
                dv = dv + more[1]
            dk_s[a] += dk
            dv_s[a] += dv

        for r in range(REACH):
            rows = pl.ds(tok + r * NODE_LEN, NODE_LEN)
            back_out[a, r, 0] = (dk_s[a, rows] * scale).astype(jnp.bfloat16)
            back_out[a, r, 1] = dv_s[a, rows].astype(jnp.bfloat16)
            back(a, r).start()
        store_query(a).start()

    for a in range(KVH):
        at = slice(a * HD, (a + 1) * HD)
        dk = dk_s[a, 0:tok] * scale
        dv = dv_s[a, 0:tok]
        dk_o[NODE_LEN:tok, at] = dk[NODE_LEN:].astype(jnp.bfloat16)
        dv_o[NODE_LEN:tok, at] = dv[NODE_LEN:].astype(jnp.bfloat16)
        dk, dv = dk[:NODE_LEN], dv[:NODE_LEN]
        for r in range(REACH):
            back(a, r).wait()
            dk = dk + back_in[a, r, 0].astype(jnp.float32)
            dv = dv + back_in[a, r, 1].astype(jnp.float32)
        dk_o[0:NODE_LEN, at] = dk.astype(jnp.bfloat16)
        dv_o[0:NODE_LEN, at] = dv.astype(jnp.bfloat16)
    last_k = pltpu.make_async_copy(dk_o, dk_hbm, out_sem.at[KVH])
    last_v = pltpu.make_async_copy(dv_o, dv_hbm, out_sem.at[KVH + 1])
    last_k.start()
    last_v.start()
    for a in range(KVH):
        store_query(a).wait()
    last_k.wait()
    last_v.wait()


def shards(queries, keys, values, out_grad, branch_ids, node_use):
    tok = queries.shape[0]
    every = tok + REACH * NODE_LEN
    low = jnp.bfloat16
    dma = pltpu.SemaphoreType.DMA
    anywhere = pl.BlockSpec(memory_space=pl.ANY)
    flops = 5 * 2 * tok * every * H * HD
    return pl.pallas_call(
        kernel,
        out_shape=(
            jax.ShapeDtypeStruct(queries.shape, low),
            jax.ShapeDtypeStruct(keys.shape, low),
            jax.ShapeDtypeStruct(values.shape, low),
        ),
        in_specs=[anywhere] * 4
        + [pl.BlockSpec(memory_space=pltpu.VMEM), pl.BlockSpec(memory_space=pltpu.SMEM)],
        out_specs=(anywhere,) * 3,
        scratch_shapes=[
            pltpu.VMEM((tok, H * HD), low),
            pltpu.VMEM((tok, H * HD), low),
            pltpu.VMEM((tok, H * HD), low),
            pltpu.VMEM((KVH, every, HD), low),
            pltpu.VMEM((KVH, every, HD), low),
            pltpu.VMEM((KVH, every, HD), jnp.float32),
            pltpu.VMEM((KVH, every, HD), jnp.float32),
            pltpu.VMEM((every, tok), jnp.float32),
            pltpu.VMEM((KVH, REACH, 2, NODE_LEN, HD), low),
            pltpu.VMEM((KVH, REACH, 2, NODE_LEN, HD), low),
            pltpu.VMEM((tok, KVH * HD), low),
            pltpu.VMEM((tok, KVH * HD), low),
            dma((4, KVH)),
            dma((KVH + 2,)),
            dma((KVH, REACH)),
            dma((KVH, REACH)),
            dma((KVH, REACH)),
            dma((KVH, REACH)),
            dma((KVH, REACH)),
            dma((KVH, REACH)),
        ],
        compiler_params=pltpu.CompilerParams(
            collective_id=0, has_side_effects=True, vmem_limit_bytes=48 * 1024 * 1024
        ),
        cost_estimate=pl.CostEstimate(
            flops=flops, bytes_accessed=8 * 1024 * 1024, transcendentals=tok * every * H
        ),
    )(queries, keys, values, out_grad, branch_ids, node_use)


def solution(mesh):
    rows = P(("group", "dp"), None)
    return jax.shard_map(
        shards,
        mesh=mesh,
        in_specs=(rows, rows, rows, rows, rows, P(("group", "dp"), None, None)),
        out_specs=(rows, rows, rows),
        check_vma=False,
    )
```

time: 151 us -> 58.8 us (0.39)
  matrix products: 57.2 us -> 0 us
  Pallas kernels: 0 us -> 50.3 us
  other arithmetic: 35.6 us -> 0 us
  local copies, waits for them, and re-layouts: 30.9 us -> 7.57 us
  starting transfers between devices: 21.5 us -> 0 us
  waiting for transfers between devices: 4.04 us -> 0 us
    dot_general x6 -> x0, matrix products: 57.2 us -> none  [the longest x1 17.2 us: attention_backward(): jnp.einsum('tkgd,skd->kgts', grad_four, value_three, preferred_element_ty...]
    pallas_call x0 -> x1, Pallas kernels: none -> 50.3 us  [shards(): pl.pallas_call(kernel, out_shape=(jax.ShapeDtypeStruct(queries.shape, low...]
    convert_element_type x1 -> x0, other arithmetic: 21.7 us -> none  [attention_backward(): dscore = (weights * (dprob - delta)).astype(jnp.bfloat16)]
    ppermute x16 -> x0, starting transfers between devices: 21.5 us -> none  [from_behind(): return lax.ppermute(value, axis, pairs)]
    reduce_sum x1 -> x0, other arithmetic: 11.1 us -> none  [attention_backward(): norm_log = jax.nn.logsumexp(scores, axis=-1, keepdims=True)]
    reshape x2 -> x0, local copies, waits for them, and re-layouts: 7.35 us -> none  [the longest x1 4.08 us: attention_backward(): grad_four = out_grad.reshape(tok_count, KVH, groups, HD)]
    slice x8 -> x0, local copies, waits for them, and re-layouts: 6.7 us -> none  [the longest x2 2.53 us: shards(): value_terms[:tok_count].at[:NODE_LEN].add(carry_value).astype(jnp.bfloat16)]
    ppermute x16 -> x0, waiting for transfers between devices: 4.04 us -> none  [from_behind(): return lax.ppermute(value, axis, pairs)]
  transfers between devices with their start and end apart: 16 -> 0, of which waited for: 2 -> 0; matrix products, arithmetic and copies ran while one was open for 40% -> 0% of each run, Pallas kernels for 0% -> 0%
where the time goes in v1:
time: 58.8 us; the launch traced here: 58.5 us
  Pallas kernels  50.3 us (86%)
  local copies, waits for them, and re-layouts  7.57 us (13%)
  between operations  0.65 us (1%)
    pallas_call x1, Pallas kernels, shards(): pl.pallas_call(kernel, out_shape=(jax.ShapeDtypeStruct(queries.shape, low...  50.3 us
    unnamed x13, local copies, waits for them, and re-layouts  7.57 us

profile of v1, /device:TPU:0, one launch (start us, length us, event | category | flops | bytes accessed | tf_op | source)
XLA Modules:
  0.0 58.5 jit_solution(4347261166753579989)
XLA Ops:
  0.6 0.0 copy-start
  0.6 1.6 %copy-done = bf16[256,4096]{1,0:T(8,128)(2,1)S(1)} copy-done((bf16[256,4096]{1,0:T(8,128)(2,1)S(1)}, bf16[256,4096]{1,0:T(8,128)(2,1)}, u32[]{:S(2)}) %copy-start) | copy-done | bytes 2097176
  2.2 0.0 copy-start.1
  2.2 0.9 %copy-done.1 = bf16[256,512]{1,0:T(8,128)(2,1)S(1)} copy-done((bf16[256,512]{1,0:T(8,128)(2,1)S(1)}, bf16[256,512]{1,0:T(8,128)(2,1)}, u32[]{:S(2)}) %copy-start.1) | copy-done | bytes 262168
  3.2 0.0 copy-start.2
  3.2 0.9 %copy-done.2 = bf16[256,512]{1,0:T(8,128)(2,1)S(1)} copy-done((bf16[256,512]{1,0:T(8,128)(2,1)S(1)}, bf16[256,512]{1,0:T(8,128)(2,1)}, u32[]{:S(2)}) %copy-start.2) | copy-done | bytes 262168
  4.1 0.0 copy-start.3
  4.1 0.7 %copy-done.3 = s32[1,4,4]{2,1,0:T(4,128)S(1)} copy-done((s32[1,4,4]{2,1,0:T(4,128)S(1)}, s32[1,4,4]{2,1,0:T(4,128)}, u32[]{:S(2)}) %copy-start.3) | copy-done | bytes 88
  4.8 0.0 copy-start.4
  4.8 0.7 %copy-done.4 = s32[1,256]{1,0:T(1,128)S(1)} copy-done((s32[1,256]{1,0:T(1,128)S(1)}, s32[1,256]{1,0:T(1,128)}, u32[]{:S(2)}) %copy-start.4) | copy-done | bytes 1048
  5.5 50.3 %shard_map.85 = (bf16[256,4096]{1,0:T(8,128)(2,1)S(1)}, bf16[256,512]{1,0:T(8,128)(2,1)S(1)}, bf16[256,512]{1,0:T(8,128)(2,1)S(1)}) custom-call(bf16[256,4096]{1,0:T(8,128)(2,1)S(1)} %copy-done, bf16[256,512]{1,0:T(8,128)(2,1)S(1)} %copy-done.1, bf16[256,512]{1,0:T(8,128)(2,1)S(1)} %copy-done.2, bf16[256,4096]{1,0:T(8,128)(2,1)} %g_hbm.1, ...), custom_call_target="tpu_custom_call" | custom-call | flops 8053063680 | bytes 8388608 | tf_op jit(solution)/shard_map/pallas_call | solution.py:204
  55.8 1.3 %copy.12 = bf16[256,4096]{1,0:T(8,128)(2,1)} copy(bf16[256,4096]{1,0:T(8,128)(2,1)S(1)} %get-tuple-element.6) | data formatting | bytes 4194304
  57.1 0.7 %copy.13 = bf16[256,512]{1,0:T(8,128)(2,1)} copy(bf16[256,512]{1,0:T(8,128)(2,1)S(1)} %get-tuple-element.7) | data formatting | bytes 524288
  57.8 0.7 %copy.14 = bf16[256,512]{1,0:T(8,128)(2,1)} copy(bf16[256,512]{1,0:T(8,128)(2,1)S(1)} %get-tuple-element.8) | data formatting | bytes 524288
Async XLA Ops:
  0.6 1.6 %copy-start = (bf16[256,4096]{1,0:T(8,128)(2,1)S(1)}, bf16[256,4096]{1,0:T(8,128)(2,1)}, u32[]{:S(2)}) copy-start(bf16[256,4096]{1,0:T(8,128)(2,1)} %q_hbm.1) | copy-start | bytes 6291460
  2.2 0.9 %copy-start.1 = (bf16[256,512]{1,0:T(8,128)(2,1)S(1)}, bf16[256,512]{1,0:T(8,128)(2,1)}, u32[]{:S(2)}) copy-start(bf16[256,512]{1,0:T(8,128)(2,1)} %k_hbm.1) | copy-start | bytes 786436
  3.2 0.9 %copy-start.2 = (bf16[256,512]{1,0:T(8,128)(2,1)S(1)}, bf16[256,512]{1,0:T(8,128)(2,1)}, u32[]{:S(2)}) copy-start(bf16[256,512]{1,0:T(8,128)(2,1)} %v_hbm.1) | copy-start | bytes 786436
  4.1 0.7 %copy-start.3 = (s32[1,4,4]{2,1,0:T(4,128)S(1)}, s32[1,4,4]{2,1,0:T(4,128)}, u32[]{:S(2)}) copy-start(s32[1,4,4]{2,1,0:T(4,128)} %use_ref.1) | copy-start | bytes 196
  4.8 0.7 %copy-start.4 = (s32[1,256]{1,0:T(1,128)S(1)}, s32[1,256]{1,0:T(1,128)}, u32[]{:S(2)}) copy-start(s32[1,256]{1,0:T(1,128)} %branch_ref.1) | copy-start | bytes 3076

commit v2 on v1

--- a/solution.py
+++ b/solution.py
@@ -14,7 +14,7 @@
 REACH = 4
 SEGS = 4
 GROUPS = H // KVH
-UNROLL = 2
+UNROLL = 8
 HIDDEN = -1e30
 MESH = pl.DeviceIdType.MESH
 
@@ -70,12 +70,9 @@
         )
 
     def forward(a, r, which):
-        source, target, send, recv = (
-            (k_hbm, k_s, k_send, k_recv),
-            (v_hbm, v_s, v_send, v_recv),
-        )[which]
+        target, send, recv = ((k_s, k_send, k_recv), (v_s, v_send, v_recv))[which]
         return pltpu.make_async_remote_copy(
-            src_ref=source.at[pl.ds(0, NODE_LEN), cols(a, HD)],
+            src_ref=target.at[a, pl.ds(0, NODE_LEN)],
             dst_ref=target.at[a, pl.ds(tok + r * NODE_LEN, NODE_LEN)],
             send_sem=send.at[a, r],
             recv_sem=recv.at[a, r],
@@ -100,7 +97,7 @@
 
     @pl.loop(0, KVH)
     def _(a):
-        for which in range(4):
+        for which in (2, 3, 0, 1):
             load(a, which).start()
 
     barrier = pltpu.get_barrier_semaphore()
@@ -111,6 +108,8 @@
 
     @pl.loop(0, KVH)
     def _(a):
+        for which in range(2):
+            load(a, which + 2).wait()
         for r in range(REACH):
             for which in range(2):
                 forward(a, r, which).start()
@@ -119,7 +118,7 @@
 
     @pl.loop(0, KVH)
     def _(a):
-        for which in range(4):
+        for which in range(2):
             load(a, which).wait()
         for r in range(REACH):
             for which in range(2):

time: 58.8 us -> 55.8 us (0.949)
  Pallas kernels: 50.3 us -> 47.3 us
    pallas_call x1, Pallas kernels: 50.3 us -> 47.3 us  [shards(): pl.pallas_call(kernel, out_shape=(jax.ShapeDtypeStruct(queries.shape, low...]
where the time goes in v2:
time: 55.8 us; the launch traced here: 55.5 us
  Pallas kernels  47.3 us (85%)
  local copies, waits for them, and re-layouts  7.57 us (14%)
  between operations  0.65 us (1%)
    pallas_call x1, Pallas kernels, shards(): pl.pallas_call(kernel, out_shape=(jax.ShapeDtypeStruct(queries.shape, low...  47.3 us
    unnamed x13, local copies, waits for them, and re-layouts  7.57 us

profile of v2, /device:TPU:0, one launch (start us, length us, event | category | flops | bytes accessed | tf_op | source)
XLA Modules:
  0.0 55.5 jit_solution(7297315091842964031)
XLA Ops:
  0.6 0.0 copy-start
  0.6 1.6 %copy-done = bf16[256,4096]{1,0:T(8,128)(2,1)S(1)} copy-done((bf16[256,4096]{1,0:T(8,128)(2,1)S(1)}, bf16[256,4096]{1,0:T(8,128)(2,1)}, u32[]{:S(2)}) %copy-start) | copy-done | bytes 2097176
  2.2 0.0 copy-start.1
  2.2 0.9 %copy-done.1 = bf16[256,512]{1,0:T(8,128)(2,1)S(1)} copy-done((bf16[256,512]{1,0:T(8,128)(2,1)S(1)}, bf16[256,512]{1,0:T(8,128)(2,1)}, u32[]{:S(2)}) %copy-start.1) | copy-done | bytes 262168
  3.2 0.0 copy-start.2
  3.2 0.9 %copy-done.2 = bf16[256,512]{1,0:T(8,128)(2,1)S(1)} copy-done((bf16[256,512]{1,0:T(8,128)(2,1)S(1)}, bf16[256,512]{1,0:T(8,128)(2,1)}, u32[]{:S(2)}) %copy-start.2) | copy-done | bytes 262168
  4.1 0.0 copy-start.3
  4.1 0.7 %copy-done.3 = s32[1,4,4]{2,1,0:T(4,128)S(1)} copy-done((s32[1,4,4]{2,1,0:T(4,128)S(1)}, s32[1,4,4]{2,1,0:T(4,128)}, u32[]{:S(2)}) %copy-start.3) | copy-done | bytes 88
  4.8 0.0 copy-start.4
  4.8 0.7 %copy-done.4 = s32[1,256]{1,0:T(1,128)S(1)} copy-done((s32[1,256]{1,0:T(1,128)S(1)}, s32[1,256]{1,0:T(1,128)}, u32[]{:S(2)}) %copy-start.4) | copy-done | bytes 1048
  5.5 47.3 %shard_map.85 = (bf16[256,4096]{1,0:T(8,128)(2,1)S(1)}, bf16[256,512]{1,0:T(8,128)(2,1)S(1)}, bf16[256,512]{1,0:T(8,128)(2,1)S(1)}) custom-call(bf16[256,4096]{1,0:T(8,128)(2,1)S(1)} %copy-done, bf16[256,512]{1,0:T(8,128)(2,1)S(1)} %copy-done.1, bf16[256,512]{1,0:T(8,128)(2,1)S(1)} %copy-done.2, bf16[256,4096]{1,0:T(8,128)(2,1)} %g_hbm.1, ...), custom_call_target="tpu_custom_call" | custom-call | flops 8053063680 | bytes 8388608 | tf_op jit(solution)/shard_map/pallas_call | solution.py:203
  52.8 1.3 %copy.12 = bf16[256,4096]{1,0:T(8,128)(2,1)} copy(bf16[256,4096]{1,0:T(8,128)(2,1)S(1)} %get-tuple-element.6) | data formatting | bytes 4194304
  54.1 0.7 %copy.13 = bf16[256,512]{1,0:T(8,128)(2,1)} copy(bf16[256,512]{1,0:T(8,128)(2,1)S(1)} %get-tuple-element.7) | data formatting | bytes 524288
  54.8 0.7 %copy.14 = bf16[256,512]{1,0:T(8,128)(2,1)} copy(bf16[256,512]{1,0:T(8,128)(2,1)S(1)} %get-tuple-element.8) | data formatting | bytes 524288
Async XLA Ops:
  0.6 1.6 %copy-start = (bf16[256,4096]{1,0:T(8,128)(2,1)S(1)}, bf16[256,4096]{1,0:T(8,128)(2,1)}, u32[]{:S(2)}) copy-start(bf16[256,4096]{1,0:T(8,128)(2,1)} %q_hbm.1) | copy-start | bytes 6291460
  2.2 0.9 %copy-start.1 = (bf16[256,512]{1,0:T(8,128)(2,1)S(1)}, bf16[256,512]{1,0:T(8,128)(2,1)}, u32[]{:S(2)}) copy-start(bf16[256,512]{1,0:T(8,128)(2,1)} %k_hbm.1) | copy-start | bytes 786436
  3.2 0.9 %copy-start.2 = (bf16[256,512]{1,0:T(8,128)(2,1)S(1)}, bf16[256,512]{1,0:T(8,128)(2,1)}, u32[]{:S(2)}) copy-start(bf16[256,512]{1,0:T(8,128)(2,1)} %v_hbm.1) | copy-start | bytes 786436
  4.1 0.7 %copy-start.3 = (s32[1,4,4]{2,1,0:T(4,128)S(1)}, s32[1,4,4]{2,1,0:T(4,128)}, u32[]{:S(2)}) copy-start(s32[1,4,4]{2,1,0:T(4,128)} %use_ref.1) | copy-start | bytes 196
  4.8 0.7 %copy-start.4 = (s32[1,256]{1,0:T(1,128)S(1)}, s32[1,256]{1,0:T(1,128)}, u32[]{:S(2)}) copy-start(s32[1,256]{1,0:T(1,128)} %branch_ref.1) | copy-start | bytes 3076

commit v3 on v2

--- a/solution.py
+++ b/solution.py
@@ -15,6 +15,7 @@
 SEGS = 4
 GROUPS = H // KVH
 UNROLL = 8
+SPAN = 1
 HIDDEN = -1e30
 MESH = pl.DeviceIdType.MESH
 
@@ -27,22 +28,22 @@
     key_at = lax.broadcasted_iota(jnp.int32, (tok, tok), 0)
     query_at = lax.broadcasted_iota(jnp.int32, (tok, tok), 1)
     local = (key_branch == query_branch) & (key_at <= query_at)
-    bias[0:tok, :] = jnp.where(local, 0.0, HIDDEN)
+    bias[...] = jnp.where(local, 0.0, HIDDEN)
+    lines = []
     for r in range(REACH):
         flag = jnp.zeros((1, tok), jnp.int32)
         for slot in range(SEGS):
             flag = jnp.where(row == slot, use_ref[0, slot, r], flag)
         line = jnp.where(flag > 0, 0.0, HIDDEN).astype(jnp.float32)
-        bias[tok + r * NODE_LEN : tok + (r + 1) * NODE_LEN, :] = jnp.broadcast_to(
-            line, (NODE_LEN, tok)
-        )
+        lines.append(line)
+    return lines
 
 
 def kernel(
     q_hbm, k_hbm, v_hbm, g_hbm, branch_ref, use_ref,
     dq_hbm, dk_hbm, dv_hbm,
-    q_s, g_s, dq_s, k_s, v_s, dk_s, dv_s, bias, back_out, back_in, dk_o, dv_o,
-    in_sem, out_sem, k_send, k_recv, v_send, v_recv, back_send, back_recv,
+    q_s, g_s, dq_s, kv_s, dk_s, dv_s, bias, back_out, back_in, dk_o, dv_o,
+    in_sem, out_sem, kv_send, kv_recv, back_send, back_recv,
 ):
     count = lax.axis_size("dp")
     me = lax.axis_index("dp")
@@ -64,18 +65,19 @@
             return pltpu.make_async_copy(
                 source.at[:, cols(a, wide)], target.at[:, cols(a, wide)], in_sem.at[which, a]
             )
-        source, target = ((k_hbm, k_s), (v_hbm, v_s))[which - 2]
         return pltpu.make_async_copy(
-            source.at[:, cols(a, HD)], target.at[a, pl.ds(0, tok)], in_sem.at[which, a]
-        )
-
-    def forward(a, r, which):
-        target, send, recv = ((k_s, k_send, k_recv), (v_s, v_send, v_recv))[which]
+            (k_hbm, v_hbm)[which - 2].at[:, cols(a, HD)],
+            kv_s.at[a, which - 2, pl.ds(0, tok)],
+            in_sem.at[which, a],
+        )
+
+    def forward(part, r):
+        heads = pl.ds(part * SPAN, SPAN)
         return pltpu.make_async_remote_copy(
-            src_ref=target.at[a, pl.ds(0, NODE_LEN)],
-            dst_ref=target.at[a, pl.ds(tok + r * NODE_LEN, NODE_LEN)],
-            send_sem=send.at[a, r],
-            recv_sem=recv.at[a, r],
+            src_ref=kv_s.at[heads, :, pl.ds(0, NODE_LEN)],
+            dst_ref=kv_s.at[heads, :, pl.ds(tok + r * NODE_LEN, NODE_LEN)],
+            send_sem=kv_send.at[part, r],
+            recv_sem=kv_recv.at[part, r],
             device_id=ahead(r + 1),
             device_id_type=MESH,
         )
@@ -106,27 +108,30 @@
             pl.semaphore_signal(barrier, inc=1, device_id=ahead(side), device_id_type=MESH)
     pl.semaphore_wait(barrier, 2 * REACH)
 
-    @pl.loop(0, KVH)
-    def _(a):
-        for which in range(2):
-            load(a, which + 2).wait()
+    @pl.loop(0, KVH // SPAN)
+    def _(part):
+        for i in range(SPAN):
+            for which in range(2):
+                load(part * SPAN + i, which + 2).wait()
         for r in range(REACH):
-            for which in range(2):
-                forward(a, r, which).start()
-
-    fill_bias(branch_ref, use_ref, bias)
+            forward(part, r).start()
+
+    lines = fill_bias(branch_ref, use_ref, bias)
 
     @pl.loop(0, KVH)
     def _(a):
         for which in range(2):
             load(a, which).wait()
-        for r in range(REACH):
-            for which in range(2):
-                forward(a, r, which).wait()
+
+        @pl.when(lax.rem(a, SPAN) == 0)
+        def _():
+            for r in range(REACH):
+                forward(a // SPAN, r).wait()
+
         dk_s[a] = jnp.zeros(dk_s.shape[1:], jnp.float32)
         dv_s[a] = jnp.zeros(dv_s.shape[1:], jnp.float32)
-        key = k_s[a]
-        value = v_s[a]
+        key = kv_s[a, 0]
+        value = kv_s[a, 1]
         key_turned = key.T
 
         def one_head(b):
@@ -136,12 +141,21 @@
             scores = lax.dot_general(
                 key, query, (((1,), (1,)), ((), ())), preferred_element_type=jnp.float32
             )
-            scores = scores * scale2 + bias[...]
             dprob = lax.dot_general(
                 value, grad, (((1,), (1,)), ((), ())), preferred_element_type=jnp.float32
             )
-            top = jnp.max(scores, axis=0, keepdims=True)
-            power = jnp.exp2(scores - top)
+            local = scores[:tok] * scale2 + bias[...]
+            nodes = [scores[tok + r * NODE_LEN : tok + (r + 1) * NODE_LEN] for r in range(REACH)]
+            top = jnp.max(local, axis=0, keepdims=True)
+            for node, line in zip(nodes, lines):
+                top = jnp.maximum(top, jnp.max(node, axis=0, keepdims=True) * scale2 + line)
+            power = jnp.exp2(
+                jnp.concatenate(
+                    [local - top]
+                    + [node * scale2 + (line - top) for node, line in zip(nodes, lines)],
+                    axis=0,
+                )
+            )
             total = jnp.sum(power, axis=0, keepdims=True)
             share = 1.0 / total
             delta = jnp.sum(power * dprob, axis=0, keepdims=True) * share
@@ -214,21 +228,18 @@
             pltpu.VMEM((tok, H * HD), low),
             pltpu.VMEM((tok, H * HD), low),
             pltpu.VMEM((tok, H * HD), low),
-            pltpu.VMEM((KVH, every, HD), low),
-            pltpu.VMEM((KVH, every, HD), low),
+            pltpu.VMEM((KVH, 2, every, HD), low),
             pltpu.VMEM((KVH, every, HD), jnp.float32),
             pltpu.VMEM((KVH, every, HD), jnp.float32),
-            pltpu.VMEM((every, tok), jnp.float32),
+            pltpu.VMEM((tok, tok), jnp.float32),
             pltpu.VMEM((KVH, REACH, 2, NODE_LEN, HD), low),
             pltpu.VMEM((KVH, REACH, 2, NODE_LEN, HD), low),
             pltpu.VMEM((tok, KVH * HD), low),
             pltpu.VMEM((tok, KVH * HD), low),
             dma((4, KVH)),
             dma((KVH + 2,)),
-            dma((KVH, REACH)),
-            dma((KVH, REACH)),
-            dma((KVH, REACH)),
-            dma((KVH, REACH)),
+            dma((KVH // SPAN, REACH)),
+            dma((KVH // SPAN, REACH)),
             dma((KVH, REACH)),
             dma((KVH, REACH)),
         ],

time: 55.8 us -> 55.5 us (level)
  no operation moved by 1% of the time
where the time goes in v3:
time: 55.5 us; the launch traced here: 55.3 us
  Pallas kernels  47.1 us (85%)
  local copies, waits for them, and re-layouts  7.57 us (14%)
  between operations  0.65 us (1%)
    pallas_call x1, Pallas kernels, shards(): pl.pallas_call(kernel, out_shape=(jax.ShapeDtypeStruct(queries.shape, low...  47.1 us
    unnamed x13, local copies, waits for them, and re-layouts  7.57 us

profile of v3, /device:TPU:0, one launch (start us, length us, event | category | flops | bytes accessed | tf_op | source)
XLA Modules:
  0.0 55.3 jit_solution(13752146602629203294)
XLA Ops:
  0.6 0.0 copy-start
  0.6 1.6 %copy-done = bf16[256,4096]{1,0:T(8,128)(2,1)S(1)} copy-done((bf16[256,4096]{1,0:T(8,128)(2,1)S(1)}, bf16[256,4096]{1,0:T(8,128)(2,1)}, u32[]{:S(2)}) %copy-start) | copy-done | bytes 2097176
  2.2 0.0 copy-start.1
  2.2 0.9 %copy-done.1 = bf16[256,512]{1,0:T(8,128)(2,1)S(1)} copy-done((bf16[256,512]{1,0:T(8,128)(2,1)S(1)}, bf16[256,512]{1,0:T(8,128)(2,1)}, u32[]{:S(2)}) %copy-start.1) | copy-done | bytes 262168
  3.2 0.0 copy-start.2
  3.2 0.9 %copy-done.2 = bf16[256,512]{1,0:T(8,128)(2,1)S(1)} copy-done((bf16[256,512]{1,0:T(8,128)(2,1)S(1)}, bf16[256,512]{1,0:T(8,128)(2,1)}, u32[]{:S(2)}) %copy-start.2) | copy-done | bytes 262168
  4.1 0.0 copy-start.3
  4.1 0.7 %copy-done.3 = s32[1,4,4]{2,1,0:T(4,128)S(1)} copy-done((s32[1,4,4]{2,1,0:T(4,128)S(1)}, s32[1,4,4]{2,1,0:T(4,128)}, u32[]{:S(2)}) %copy-start.3) | copy-done | bytes 88
  4.8 0.0 copy-start.4
  4.8 0.7 %copy-done.4 = s32[1,256]{1,0:T(1,128)S(1)} copy-done((s32[1,256]{1,0:T(1,128)S(1)}, s32[1,256]{1,0:T(1,128)}, u32[]{:S(2)}) %copy-start.4) | copy-done | bytes 1048
  5.5 47.1 %shard_map.85 = (bf16[256,4096]{1,0:T(8,128)(2,1)S(1)}, bf16[256,512]{1,0:T(8,128)(2,1)S(1)}, bf16[256,512]{1,0:T(8,128)(2,1)S(1)}) custom-call(bf16[256,4096]{1,0:T(8,128)(2,1)S(1)} %copy-done, bf16[256,512]{1,0:T(8,128)(2,1)S(1)} %copy-done.1, bf16[256,512]{1,0:T(8,128)(2,1)S(1)} %copy-done.2, bf16[256,4096]{1,0:T(8,128)(2,1)} %g_hbm.1, ...), custom_call_target="tpu_custom_call" | custom-call | flops 8053063680 | bytes 8388608 | tf_op jit(solution)/shard_map/pallas_call | solution.py:217
  52.5 1.3 %copy.12 = bf16[256,4096]{1,0:T(8,128)(2,1)} copy(bf16[256,4096]{1,0:T(8,128)(2,1)S(1)} %get-tuple-element.6) | data formatting | bytes 4194304
  53.9 0.7 %copy.13 = bf16[256,512]{1,0:T(8,128)(2,1)} copy(bf16[256,512]{1,0:T(8,128)(2,1)S(1)} %get-tuple-element.7) | data formatting | bytes 524288
  54.6 0.7 %copy.14 = bf16[256,512]{1,0:T(8,128)(2,1)} copy(bf16[256,512]{1,0:T(8,128)(2,1)S(1)} %get-tuple-element.8) | data formatting | bytes 524288
Async XLA Ops:
  0.6 1.6 %copy-start = (bf16[256,4096]{1,0:T(8,128)(2,1)S(1)}, bf16[256,4096]{1,0:T(8,128)(2,1)}, u32[]{:S(2)}) copy-start(bf16[256,4096]{1,0:T(8,128)(2,1)} %q_hbm.1) | copy-start | bytes 6291460
  2.2 0.9 %copy-start.1 = (bf16[256,512]{1,0:T(8,128)(2,1)S(1)}, bf16[256,512]{1,0:T(8,128)(2,1)}, u32[]{:S(2)}) copy-start(bf16[256,512]{1,0:T(8,128)(2,1)} %k_hbm.1) | copy-start | bytes 786436
  3.2 0.9 %copy-start.2 = (bf16[256,512]{1,0:T(8,128)(2,1)S(1)}, bf16[256,512]{1,0:T(8,128)(2,1)}, u32[]{:S(2)}) copy-start(bf16[256,512]{1,0:T(8,128)(2,1)} %v_hbm.1) | copy-start | bytes 786436
  4.1 0.7 %copy-start.3 = (s32[1,4,4]{2,1,0:T(4,128)S(1)}, s32[1,4,4]{2,1,0:T(4,128)}, u32[]{:S(2)}) copy-start(s32[1,4,4]{2,1,0:T(4,128)} %use_ref.1) | copy-start | bytes 196
  4.8 0.7 %copy-start.4 = (s32[1,256]{1,0:T(1,128)S(1)}, s32[1,256]{1,0:T(1,128)}, u32[]{:S(2)}) copy-start(s32[1,256]{1,0:T(1,128)} %branch_ref.1) | copy-start | bytes 3076
